TPU v7x, 256 devices: a whole 4x4x8 slice. The times are simulated.
256 devices in a mesh: gx: 8 (over y, z_lo), gy: 8 (over x, core), gz: 4 (over z_hi).
Axes of the slice: x: 4, y: 4, z: 8 (z_hi: 4, z_lo: 2; z = z_hi * 2 + z_lo), core: 2. Of those that a mesh axis runs over, the one named last changes fastest.
Arguments:
- coefficients: bfloat16 [262144, 16, 128], P(('gx', 'gy', 'gz')), may hold values from -6 to 6
- translations: bfloat16 [4, 2, 2, 128, 128], replicated, may hold values from -0.375 to 0.375
- box_gains: bfloat16 [4, 262144, 128], P(None, ('gx', 'gy', 'gz')), may hold values from 0.25 to 1.75
Outputs:
- result: bfloat16 [262144, 16, 128], P(('gx', 'gy', 'gz'))
All inputs are finite; a program needn't handle non-finite values.
Results may differ from a plain program's by a relative error of at most 0.0064.
Values may be sent and summed in bfloat16 or wider, within the bound.
A program may use at most 128 MiB of HBM per device.

v0:
```python
import jax
import jax.numpy as jnp
from jax import lax
from jax.sharding import PartitionSpec as P


def partner(value, axis, apart):
    mask = 2**apart
    pairs = [(source, source ^ mask) for source in range(lax.axis_size(axis))]
    return lax.ppermute(value, axis, pairs)


def split_halves(current, side_bit):
    half_rows = current.shape[0] // 2
    kept_rows = lax.dynamic_slice_in_dim(current, side_bit * half_rows, half_rows, 0)
    given_rows = lax.dynamic_slice_in_dim(current, (1 - side_bit) * half_rows, half_rows, 0)
    return (kept_rows, given_rows)


def combine(kept_rows, other_rows, side_bit, level_blocks, level_gains):
    row_count = kept_rows.shape[0] * kept_rows.shape[1]
    joined = jnp.concatenate(
        [kept_rows.reshape(row_count, -1), other_rows.reshape(row_count, -1)], axis=1
    )
    select_self = lax.dynamic_index_in_dim(level_blocks, side_bit, 1, keepdims=False)
    select_other = lax.dynamic_index_in_dim(level_blocks, 1 - side_bit, 1, keepdims=False)
    results = []
    for target in range(2):
        stacked = jnp.concatenate([select_self[target], select_other[target]], axis=0)
        results.append(
            jnp.dot(joined, stacked, preferred_element_type=jnp.float32).reshape(kept_rows.shape)
        )
    total = jnp.concatenate(results, axis=0)
    return (total * level_gains[:, None, :].astype(jnp.float32)).astype(jnp.bfloat16)


def middle_level(current, bit_number, section_index, translations, box_gains):
    side_bit = lax.axis_index(("gy", "gz")) >> bit_number & 1
    kept_rows, given_rows = split_halves(current, side_bit)
    arrived = partner(given_rows, ("gy", "gz"), bit_number)
    return combine(
        kept_rows, arrived, side_bit, translations[section_index], box_gains[section_index]
    )


def shards(coefficients, translations, box_gains):
    side_bit = lax.axis_index("gx") & 1
    kept_rows, given_rows = split_halves(coefficients, side_bit)
    arrived = partner(given_rows, "gx", 0)
    current = combine(kept_rows, arrived, side_bit, translations[0], box_gains[0])
    current = middle_level(current, 0, 1, translations, box_gains)
    current = middle_level(current, 1, 2, translations, box_gains)
    current = middle_level(current, 2, 3, translations, box_gains)
    return current


def solution(mesh):
    return jax.shard_map(
        shards,
        mesh=mesh,
        in_specs=(P(("gx", "gy", "gz"), None, None), P(), P(None, ("gx", "gy", "gz"), None)),
        out_specs=P(("gx", "gy", "gz"), None, None),
        check_vma=False,
    )
```

profile of v0, /device:TPU:1, one launch (start us, length us, event | category | flops | bytes accessed | tf_op | source)
XLA Modules:
  0.0 283.6 jit_solution(6672073872259935997)
XLA Ops:
  0.0 0.0 copy-start.1
  0.0 4.3 %constant_dynamic-slice_fusion.7 = (bf16[512,16,128]{2,1,0:T(8,128)(2,1)S(1)}, bf16[512,16,128]{2,1,0:T(8,128)(2,1)}) fusion(bf16[1024,16,128]{2,1,0:T(8,128)(2,1)} %param.3, s32[]{:T(128)S(6)} %select_n.49, s32[]{:T(128)S(6)} %select_n.50), kind=kLoop, calls=%fused_computation.71 | loop fusion | bytes 8388616 | tf_op jit(solution)/shard_map/dynamic_slice | solution.py:15
  4.3 2.5 collective-permute-start
  6.8 0.0 copy-done.1
  6.9 2.1 bitcast_convert_fusion
  9.0 42.4 %collective-permute-done = bf16[512,16,128]{2,1,0:T(8,128)(2,1)} collective-permute-done((bf16[512,16,128]{2,1,0:T(8,128)(2,1)}, bf16[512,16,128]{2,1,0:T(8,128)(2,1)}, u32[]{:S(2)}, u32[]{:S(2)}) %collective-permute-start) | collective-permute-done | bytes 2097184 | tf_op jit(solution)/shard_map/ppermute | solution.py:10
  51.4 2.8 fusion.11
  54.2 2.8 fusion.10
  57.1 1.1 fusion
  58.2 2.0 constant_dynamic-slice_fusion.5
  60.3 3.9 %collective-permute-start.1 = (bf16[512,16,128]{2,1,0:T(8,128)(2,1)}, bf16[512,16,128]{2,1,0:T(8,128)(2,1)}, u32[]{:S(2)}, u32[]{:S(2)}) collective-permute-start(bf16[512,16,128]{2,1,0:T(8,128)(2,1)} %get-tuple-element.10), channel_id=1, source_target_pairs={{0,1},{1,0},{2,3},{3,2},{4,5},{5,4},{6,7},{7,6},{8,9},{9,8},{10,11... | collective-permute-start | bytes 6291464 | tf_op jit(solution)/shard_map/ppermute | solution.py:10
  64.2 90.3 %collective-permute-done.1 = bf16[512,16,128]{2,1,0:T(8,128)(2,1)} collective-permute-done((bf16[512,16,128]{2,1,0:T(8,128)(2,1)}, bf16[512,16,128]{2,1,0:T(8,128)(2,1)}, u32[]{:S(2)}, u32[]{:S(2)}) %collective-permute-start.1) | collective-permute-done | bytes 2097184 | tf_op jit(solution)/shard_map/ppermute | solution.py:10
  154.5 2.8 fusion.9
  157.3 0.0 copy-start
  157.3 2.9 %fusion.8 = f32[8192,128]{1,0:T(8,128)S(1)} fusion(bf16[8192,128]{1,0:T(8,128)(2,1)} %bitcast.10, bf16[8192,128]{1,0:T(8,128)(2,1)S(1)} %bitcast.73, bf16[128,128]{1,0:T(8,128)(2,1)S(1)} %get-tuple-element.31, bf16[128,128]{1,0:T(8,128)(2,1)S(1)} %get-tuple-element.32), kind=kOutput, calls=%fused_computation.16 | convolution fusion | flops 545390592 | bytes 8454144 | tf_op jit(solution)/shard_map/dot_general | solution.py:31
  160.2 0.0 copy-done
  160.2 1.1 fusion.1
  161.4 2.0 constant_dynamic-slice_fusion.3
  163.4 6.4 %collective-permute-start.2 = (bf16[512,16,128]{2,1,0:T(8,128)(2,1)}, bf16[512,16,128]{2,1,0:T(8,128)(2,1)}, u32[]{:S(2)}, u32[]{:S(2)}) collective-permute-start(bf16[512,16,128]{2,1,0:T(8,128)(2,1)} %get-tuple-element.8), channel_id=1, source_target_pairs={{0,2},{1,3},{2,0},{3,1},{4,6},{5,7},{6,4},{7,5},{8,10},{9,11},{10,... | collective-permute-start | bytes 6291464 | tf_op jit(solution)/shard_map/ppermute | solution.py:10
  169.9 90.7 %collective-permute-done.2 = bf16[512,16,128]{2,1,0:T(8,128)(2,1)} collective-permute-done((bf16[512,16,128]{2,1,0:T(8,128)(2,1)}, bf16[512,16,128]{2,1,0:T(8,128)(2,1)}, u32[]{:S(2)}, u32[]{:S(2)}) %collective-permute-start.2) | collective-permute-done | bytes 2097184 | tf_op jit(solution)/shard_map/ppermute | solution.py:10
  260.6 2.8 fusion.7
  263.4 2.8 fusion.6
  266.3 1.2 fusion.2
  267.4 2.0 constant_dynamic-slice_fusion.1
  269.5 1.7 collective-permute-start.3
  271.2 4.1 %collective-permute-done.3 = bf16[512,16,128]{2,1,0:T(8,128)(2,1)} collective-permute-done((bf16[512,16,128]{2,1,0:T(8,128)(2,1)}, bf16[512,16,128]{2,1,0:T(8,128)(2,1)}, u32[]{:S(2)}, u32[]{:S(2)}) %collective-permute-start.3) | collective-permute-done | bytes 2097184 | tf_op jit(solution)/shard_map/ppermute | solution.py:10
  275.3 2.8 fusion.5
  278.1 2.8 %fusion.4 = f32[8192,128]{1,0:T(8,128)S(1)} fusion(bf16[8192,128]{1,0:T(8,128)(2,1)} %bitcast.28, bf16[8192,128]{1,0:T(8,128)(2,1)S(1)} %bitcast.75, bf16[128,128]{1,0:T(8,128)(2,1)S(1)} %get-tuple-element.23, bf16[128,128]{1,0:T(8,128)(2,1)S(1)} %get-tuple-element.24), kind=kOutput, calls=%fused_computation.12 | convolution fusion | flops 545390592 | bytes 8454144 | tf_op jit(solution)/shard_map/dot_general | solution.py:31
  281.0 2.7 fusion.3
  (5 shorter events, 0.1 us)
Async XLA Ops:
  0.0 6.8 %copy-start.1 = (bf16[4,2,2,128,128]{4,3,2,1,0:T(8,128)(2,1)S(1)}, bf16[4,2,2,128,128]{4,3,2,1,0:T(8,128)(2,1)}, u32[]{:S(2)}) copy-start(bf16[4,2,2,128,128]{4,3,2,1,0:T(8,128)(2,1)} %param.4) | copy-start | bytes 1572868
  4.3 47.1 %collective-permute-start = (bf16[512,16,128]{2,1,0:T(8,128)(2,1)}, bf16[512,16,128]{2,1,0:T(8,128)(2,1)}, u32[]{:S(2)}, u32[]{:S(2)}) collective-permute-start(bf16[512,16,128]{2,1,0:T(8,128)(2,1)} %get-tuple-element.12), channel_id=1, source_target_pairs={{0,32},{32,0},{64,96},{96,64},{128,160},{160,128},{192,224},{224,1... | collective-permute-start | bytes 6291464 | tf_op jit(solution)/shard_map/ppermute | solution.py:10
  60.3 94.2 %collective-permute-start.1 = (bf16[512,16,128]{2,1,0:T(8,128)(2,1)}, bf16[512,16,128]{2,1,0:T(8,128)(2,1)}, u32[]{:S(2)}, u32[]{:S(2)}) collective-permute-start(bf16[512,16,128]{2,1,0:T(8,128)(2,1)} %get-tuple-element.10), channel_id=1, source_target_pairs={{0,1},{1,0},{2,3},{3,2},{4,5},{5,4},{6,7},{7,6},{8,9},{9,8},{10,11... | collective-permute-start | bytes 6291464 | tf_op jit(solution)/shard_map/ppermute | solution.py:10
  157.3 2.9 %copy-start = (f32[1024,128]{1,0:T(8,128)S(1)}, f32[1024,128]{1,0:T(8,128)}, u32[]{:S(2)}) copy-start(f32[1024,128]{1,0:T(8,128)} %get-tuple-element.14) | copy-start | bytes 1572868
  163.4 97.2 %collective-permute-start.2 = (bf16[512,16,128]{2,1,0:T(8,128)(2,1)}, bf16[512,16,128]{2,1,0:T(8,128)(2,1)}, u32[]{:S(2)}, u32[]{:S(2)}) collective-permute-start(bf16[512,16,128]{2,1,0:T(8,128)(2,1)} %get-tuple-element.8), channel_id=1, source_target_pairs={{0,2},{1,3},{2,0},{3,1},{4,6},{5,7},{6,4},{7,5},{8,10},{9,11},{10,... | collective-permute-start | bytes 6291464 | tf_op jit(solution)/shard_map/ppermute | solution.py:10
  269.5 5.8 %collective-permute-start.3 = (bf16[512,16,128]{2,1,0:T(8,128)(2,1)}, bf16[512,16,128]{2,1,0:T(8,128)(2,1)}, u32[]{:S(2)}, u32[]{:S(2)}) collective-permute-start(bf16[512,16,128]{2,1,0:T(8,128)(2,1)} %get-tuple-element.6), channel_id=1, source_target_pairs={{0,4},{1,5},{2,6},{3,7},{4,0},{5,1},{6,2},{7,3},{8,12},{9,13},{10,... | collective-permute-start | bytes 6291464 | tf_op jit(solution)/shard_map/ppermute | solution.py:10
where the time goes:
time: 284 us
  waiting for transfers between devices  228 us (80%)
  matrix products  22.7 us (8%)
  starting transfers between devices  14.5 us (5%)
  local copies, waits for them, and re-layouts  10.6 us (4%)
  other arithmetic  8.22 us (3%)
    ppermute x4, waiting for transfers between devices, partner(): return lax.ppermute(value, axis, pairs)  228 us
    dot_general x8, matrix products, combine(): jnp.dot(joined, stacked, preferred_element_type=jnp.float32)  22.7 us
    ppermute x4, starting transfers between devices, partner(): return lax.ppermute(value, axis, pairs)  14.5 us
    dynamic_slice x4, local copies, waits for them, and re-layouts, split_halves(): lax.dynamic_slice_in_dim(current, side_bit * half_rows, half_rows, 0)  10.5 us
    convert_element_type x4, other arithmetic, combine(): (total * level_gains[:, None, :].astype(jnp.float32)).astype(jnp.bfloat16)  6.08 us
  transfers between devices with their start and end apart: 4, of which 4 were waited for; matrix products, arithmetic and copies ran while one was open for 1% of the time, Pallas kernels for 0%

commit v1 on v0

v1 whole, which is shorter than its diff:
```python
import functools

import jax
import jax.numpy as jnp
from jax import lax
from jax.experimental import pallas as pl
from jax.experimental.pallas import tpu as pltpu
from jax.sharding import PartitionSpec as P

MESH = pl.DeviceIdType.MESH
LEVELS = 4
CHUNKS = 16
AHEAD = 3
LAGS = (0, 2, 4, 5)


def butterfly(
    coefs, blocks, gains, result,
    own, blocks_in, weights, factors, kept, given, arrived, done,
    own_sems, block_sem, gain_sems, send_sems, recv_sems, out_sems,
):
    gx, gy, gz = lax.axis_index("gx"), lax.axis_index("gy"), lax.axis_index("gz")
    sides = (gx % 2, gz % 2, gz // 2, gy % 2)
    partners = (
        {"gx": gx + 1 - 2 * sides[0]},
        {"gz": gz + 1 - 2 * sides[1]},
        {"gz": gz + 2 - 4 * sides[2]},
        {"gy": gy + 1 - 2 * sides[3]},
    )
    half, vecs, width = own.shape
    size = half // CHUNKS
    rows = size * vecs

    def part(chunk):
        return pl.ds(chunk * size, size)

    def targets(level):
        if level == LEVELS - 1:
            return (0, 1)
        return (1 - sides[level + 1], sides[level + 1])

    def load_own(chunk):
        return pltpu.make_async_copy(
            coefs.at[sides[0], part(chunk)], own.at[part(chunk)], own_sems.at[chunk]
        )

    def load_gains(level, place):
        return pltpu.make_async_copy(
            gains.at[level, targets(level)[place]], factors.at[level, place], gain_sems.at[level, place]
        )

    def exchange(level, chunk):
        if level == 0:
            source = coefs.at[1 - sides[0], part(chunk)]
        else:
            source = given.at[level - 1, part(chunk)]
        return pltpu.make_async_remote_copy(
            src_ref=source,
            dst_ref=arrived.at[level, part(chunk)],
            send_sem=send_sems.at[level, chunk],
            recv_sem=recv_sems.at[level, chunk],
            device_id=partners[level],
            device_id_type=MESH,
        )

    def store(place, chunk):
        return pltpu.make_async_copy(
            done.at[place, part(chunk)], result.at[place, part(chunk)], out_sems.at[place, chunk]
        )

    block_copy = pltpu.make_async_copy(blocks, blocks_in, block_sem)
    block_copy.start()
    for chunk in range(CHUNKS):
        load_own(chunk).start()
    for level in range(LEVELS):
        for place in range(2):
            load_gains(level, place).start()

    barrier = pltpu.get_barrier_semaphore()
    for level in range(LEVELS):
        pl.semaphore_signal(barrier, inc=1, device_id=partners[level], device_id_type=MESH)
    pl.semaphore_wait(barrier, LEVELS)

    for chunk in range(AHEAD):
        exchange(0, chunk).start()

    block_copy.wait()
    for level in range(LEVELS):
        for place in range(2):
            for origin in range(2):
                source = sides[level] if origin == 0 else 1 - sides[level]
                weights[level, pl.ds(origin * width, width), pl.ds(place * width, width)] = blocks_in[
                    level, targets(level)[place], source
                ]
    for level in range(LEVELS):
        for place in range(2):
            load_gains(level, place).wait()

    def work(level, chunk):
        here = part(chunk)
        if level == 0:
            load_own(chunk).wait()
            self_rows = own
        else:
            self_rows = kept.at[level - 1]
        exchange(level, chunk).wait_recv()
        joined = jnp.concatenate(
            [self_rows[here].reshape(rows, width), arrived[level, here].reshape(rows, width)], axis=1
        )
        total = jnp.dot(joined, weights[level], preferred_element_type=jnp.float32)
        for place in range(2):
            scale = factors[level, place, here].astype(jnp.float32)
            columns = total[:, place * width : (place + 1) * width].reshape(size, vecs, width)
            values = (columns * scale[:, None, :]).astype(jnp.bfloat16)
            if level == LEVELS - 1:
                done[place, here] = values
                store(place, chunk).start()
            elif place == 0:
                given[level, here] = values
                exchange(level + 1, chunk).start()
            else:
                kept[level, here] = values

    def step(index, carry):
        for level in range(LEVELS):
            chunk = index - LAGS[level]

            @pl.when((chunk >= 0) & (chunk < CHUNKS))
            def _(level=level, chunk=chunk):
                work(level, chunk)

            if level == 0:

                @pl.when(index + AHEAD < CHUNKS)
                def _():
                    exchange(0, index + AHEAD).start()

        return carry

    lax.fori_loop(0, CHUNKS + LAGS[-1], step, 0)

    def finish(chunk, carry):
        for level in range(LEVELS):
            exchange(level, chunk).wait_send()
        for place in range(2):
            store(place, chunk).wait()
        return carry

    lax.fori_loop(0, CHUNKS, finish, 0)


def shards(coefficients, translations, box_gains):
    boxes, vecs, width = coefficients.shape
    half = boxes // 2
    bf16 = jnp.bfloat16
    anywhere = pl.BlockSpec(memory_space=pl.ANY)
    result = pl.pallas_call(
        butterfly,
        out_shape=jax.ShapeDtypeStruct((2, half, vecs, width), bf16),
        in_specs=[anywhere] * 3,
        out_specs=anywhere,
        scratch_shapes=[
            pltpu.VMEM((half, vecs, width), bf16),
            pltpu.VMEM(translations.shape, bf16),
            pltpu.VMEM((LEVELS, 2 * width, 2 * width), bf16),
            pltpu.VMEM((LEVELS, 2, half, width), bf16),
            pltpu.VMEM((LEVELS - 1, half, vecs, width), bf16),
            pltpu.VMEM((LEVELS - 1, half, vecs, width), bf16),
            pltpu.VMEM((LEVELS, half, vecs, width), bf16),
            pltpu.VMEM((2, half, vecs, width), bf16),
            pltpu.SemaphoreType.DMA((CHUNKS,)),
            pltpu.SemaphoreType.DMA,
            pltpu.SemaphoreType.DMA((LEVELS, 2)),
            pltpu.SemaphoreType.DMA((LEVELS, CHUNKS)),
            pltpu.SemaphoreType.DMA((LEVELS, CHUNKS)),
            pltpu.SemaphoreType.DMA((2, CHUNKS)),
        ],
        compiler_params=pltpu.CompilerParams(
            collective_id=0, has_side_effects=True, vmem_limit_bytes=48 * 2**20
        ),
        cost_estimate=pl.CostEstimate(
            flops=LEVELS * 2 * half * vecs * 4 * width * width,
            bytes_accessed=10 * 2**20,
            transcendentals=0,
        ),
    )(
        coefficients.reshape(2, half, vecs, width),
        translations,
        box_gains.reshape(LEVELS, 2, half, width),
    )
    return result.reshape(boxes, vecs, width)


def solution(mesh):
    return jax.shard_map(
        shards,
        mesh=mesh,
        in_specs=(P(("gx", "gy", "gz"), None, None), P(), P(None, ("gx", "gy", "gz"), None)),
        out_specs=P(("gx", "gy", "gz"), None, None),
        check_vma=False,
    )
```

time: 284 us -> 208 us (0.73)
  waiting for transfers between devices: 228 us -> 0 us
  Pallas kernels: 0 us -> 204 us
  matrix products: 22.7 us -> 0 us
  starting transfers between devices: 14.5 us -> 0 us
  other arithmetic: 8.22 us -> 0 us
  local copies, waits for them, and re-layouts: 10.6 us -> 4.28 us
    ppermute x4 -> x0, waiting for transfers between devices: 228 us -> none  [partner(): return lax.ppermute(value, axis, pairs)]
    pallas_call x0 -> x1, Pallas kernels: none -> 204 us  [shards(): pl.pallas_call(butterfly, out_shape=jax.ShapeDtypeStruct((2, half, vecs,...]
    dot_general x8 -> x0, matrix products: 22.7 us -> none  [combine(): jnp.dot(joined, stacked, preferred_element_type=jnp.float32)]
    ppermute x4 -> x0, starting transfers between devices: 14.5 us -> none  [partner(): return lax.ppermute(value, axis, pairs)]
    dynamic_slice x4 -> x0, local copies, waits for them, and re-layouts: 10.5 us -> none  [split_halves(): lax.dynamic_slice_in_dim(current, side_bit * half_rows, half_rows, 0)]
    convert_element_type x5 -> x0, other arithmetic: 8.22 us -> none  [the longest x4 6.08 us: combine(): (total * level_gains[:, None, :].astype(jnp.float32)).astype(jnp.bfloat16)]
    unnamed x4 -> x5, local copies, waits for them, and re-layouts: 0.01 us -> 4.28 us
  transfers between devices with their start and end apart: 4 -> 0, of which waited for: 4 -> 0; matrix products, arithmetic and copies ran while one was open for 1% -> 0% of each run, Pallas kernels for 0% -> 0%
where the time goes in v1:
time: 208 us
  Pallas kernels  204 us (98%)
  local copies, waits for them, and re-layouts  4.28 us (2%)
    pallas_call x1, Pallas kernels, shards(): pl.pallas_call(butterfly, out_shape=jax.ShapeDtypeStruct((2, half, vecs,...  204 us
    unnamed x5, local copies, waits for them, and re-layouts  4.28 us

profile of v1, /device:TPU:1, one launch (start us, length us, event | category | flops | bytes accessed | tf_op | source)
XLA Modules:
  0.0 208.2 jit_solution(14366895824297042875)
XLA Ops:
  0.0 0.0 copy-start
  0.0 1.2 copy-done
  1.2 0.0 copy-start.1
  1.2 1.0 copy-done.1
  2.3 203.9 %shard_map.37 = bf16[2,512,16,128]{3,2,1,0:T(8,128)(2,1)S(1)} custom-call(bf16[2,512,16,128]{3,2,1,0:T(8,128)(2,1)} %bitcast.5, bf16[4,2,2,128,128]{4,3,2,1,0:T(8,128)(2,1)S(1)} %copy-done.1, bf16[4,2,512,128]{3,2,1,0:T(8,128)(2,1)S(1)} %bitcast.4), custom_call_target="tpu_custom_call" | custom-call | flops 4294967296 | bytes 10485760 | tf_op jit(solution)/shard_map/pallas_call | solution.py:157
  206.1 2.0 copy.5
Async XLA Ops:
  0.0 1.2 copy-start
  1.2 1.0 copy-start.1

commit v2 on v1

v2 whole, which is shorter than its diff:
```python
import functools

import jax
import jax.numpy as jnp
from jax import lax
from jax.experimental import pallas as pl
from jax.experimental.pallas import tpu as pltpu
from jax.sharding import PartitionSpec as P

MESH = pl.DeviceIdType.MESH
LEVELS = 4
SMALL = 16
LARGE = 32
HEAD = 2
TAIL = 2
FIRST = 2
AHEAD = 2
LAGS = (0, 2, 7, 9)
PASS_LAG = 4


def butterfly(
    coefs, blocks, gains, result,
    own, blocks_in, weights, factors, kept, given, arrived, passing,
    own_sem, block_sem, gain_sem, send_sems, recv_sems, pass_sems,
):
    gx, gy, gz = lax.axis_index("gx"), lax.axis_index("gy"), lax.axis_index("gz")
    sides = (gx % 2, gz % 2, gz // 2, gy % 2)
    partners = (
        {"gx": gx + 1 - 2 * sides[0]},
        {"gz": gz + 1 - 2 * sides[1]},
        {"gz": (gz + 1 + 2 * sides[3]) % 4},
        {"gy": gy + 1 - 2 * sides[3]},
    )
    half, vecs, width = own.shape
    larges = (half - (HEAD + TAIL) * SMALL) // LARGE
    chunks = larges + HEAD + TAIL

    def part(chunk, size):
        if size == LARGE:
            return pl.ds((chunk - HEAD) * LARGE + HEAD * SMALL, LARGE)
        late = (chunk + chunks - larges - HEAD) // chunks
        return pl.ds(chunk * SMALL + late * larges * (LARGE - SMALL), SMALL)

    def by_size(chunk, action):
        inner = (chunk >= HEAD) & (chunk < HEAD + larges)

        @pl.when(inner)
        def _():
            action(chunk, LARGE)

        @pl.when(jnp.logical_not(inner))
        def _():
            action(chunk, SMALL)

    def targets(level):
        if level == LEVELS - 1:
            return (0, 1)
        return (1 - sides[level + 1], sides[level + 1])

    def load_gains(level, place):
        return pltpu.make_async_copy(
            gains.at[level, targets(level)[place]], factors.at[level, place], gain_sem
        )

    def exchange(level, chunk, size):
        if level == 0:
            source = coefs.at[1 - sides[0], part(chunk, size)]
        else:
            source = given.at[level - 1, part(chunk, size)]
        return pltpu.make_async_remote_copy(
            src_ref=source,
            dst_ref=passing.at[part(chunk, size)] if level == 2 else arrived.at[level, part(chunk, size)],
            send_sem=send_sems.at[level],
            recv_sem=pass_sems.at[chunk] if level == 2 else recv_sems.at[level, chunk],
            device_id=partners[level],
            device_id_type=MESH,
        )

    def onward(chunk, size):
        return pltpu.make_async_remote_copy(
            src_ref=passing.at[part(chunk, size)],
            dst_ref=arrived.at[2, part(chunk, size)],
            send_sem=send_sems.at[LEVELS],
            recv_sem=recv_sems.at[2, chunk],
            device_id=partners[2],
            device_id_type=MESH,
        )

    own_copy = pltpu.make_async_copy(coefs.at[sides[0]], own, own_sem)
    block_copy = pltpu.make_async_copy(blocks, blocks_in, block_sem)
    block_copy.start()
    own_copy.start()
    for level in range(LEVELS):
        for place in range(2):
            load_gains(level, place).start()

    barrier = pltpu.get_barrier_semaphore()
    for peer in (partners[0], {"gz": (gz + 1) % 4}, {"gz": (gz + 3) % 4}, partners[3]):
        pl.semaphore_signal(barrier, inc=1, device_id=peer, device_id_type=MESH)
    pl.semaphore_wait(barrier, 4)

    for chunk in range(FIRST):
        exchange(0, chunk, SMALL if chunk < HEAD else LARGE).start()

    block_copy.wait()
    for level in range(LEVELS):
        for place in range(2):
            for origin in range(2):
                source = sides[level] if origin == 0 else 1 - sides[level]
                weights[level, pl.ds(origin * width, width), pl.ds(place * width, width)] = blocks_in[
                    level, targets(level)[place], source
                ]
    pltpu.make_async_copy(factors, factors, gain_sem).wait()
    own_copy.wait()

    def work(level, chunk, size):
        here = part(chunk, size)
        rows = size * vecs
        if level == 0:
            self_rows = own
        else:
            self_rows = kept.at[level - 1]
        if level == 2:
            onward(chunk, size).wait_recv()
        else:
            exchange(level, chunk, size).wait_recv()
        joined = jnp.concatenate(
            [self_rows[here].reshape(rows, width), arrived[level, here].reshape(rows, width)], axis=1
        )
        total = jnp.dot(joined, weights[level], preferred_element_type=jnp.float32)
        for place in range(2):
            scale = factors[level, place, here].astype(jnp.float32)
            columns = total[:, place * width : (place + 1) * width].reshape(size, vecs, width)
            values = (columns * scale[:, None, :]).astype(jnp.bfloat16)
            if level == LEVELS - 1:
                result[place, here] = values
            elif place == 0:
                given[level, here] = values
                exchange(level + 1, chunk, size).start()
            else:
                kept[level, here] = values

    def forward(chunk, size):
        exchange(2, chunk, size).wait_recv()
        onward(chunk, size).start()

    def when_valid(chunk, action):
        @pl.when((chunk >= 0) & (chunk < chunks))
        def _():
            by_size(chunk, action)

    def begin(chunk, size):
        exchange(0, chunk, size).start()

    def step(index, carry):
        when_valid(index, functools.partial(work, 0))
        if FIRST < AHEAD + 1:

            @pl.when(index == 0)
            def _():
                for chunk in range(FIRST, AHEAD):
                    begin(chunk, SMALL if chunk < HEAD else LARGE)

        when_valid(index + AHEAD, begin)
        when_valid(index - LAGS[1], functools.partial(work, 1))
        when_valid(index - PASS_LAG, forward)
        when_valid(index - LAGS[2], functools.partial(work, 2))
        when_valid(index - LAGS[3], functools.partial(work, 3))
        return carry

    lax.fori_loop(0, chunks + LAGS[-1], step, 0)

    for index in range(LEVELS + 1):
        pltpu.make_async_copy(arrived.at[0], arrived.at[0], send_sems.at[index]).wait()


def in_hbm(array):
    return pltpu.with_memory_space_constraint(array, pltpu.HBM)


def shards(coefficients, translations, box_gains):
    boxes, vecs, width = coefficients.shape
    half = boxes // 2
    chunks = (half - (HEAD + TAIL) * SMALL) // LARGE + HEAD + TAIL
    bf16 = jnp.bfloat16
    anywhere = pl.BlockSpec(memory_space=pltpu.HBM)
    result = pl.pallas_call(
        butterfly,
        out_shape=pltpu.VMEM((2, half, vecs, width), bf16),
        in_specs=[anywhere] * 3,
        out_specs=pl.BlockSpec(memory_space=pltpu.VMEM),
        scratch_shapes=[
            pltpu.VMEM((half, vecs, width), bf16),
            pltpu.VMEM(translations.shape, bf16),
            pltpu.VMEM((LEVELS, 2 * width, 2 * width), bf16),
            pltpu.VMEM((LEVELS, 2, half, width), bf16),
            pltpu.VMEM((LEVELS - 1, half, vecs, width), bf16),
            pltpu.VMEM((LEVELS - 1, half, vecs, width), bf16),
            pltpu.VMEM((LEVELS, half, vecs, width), bf16),
            pltpu.VMEM((half, vecs, width), bf16),
            pltpu.SemaphoreType.DMA,
            pltpu.SemaphoreType.DMA,
            pltpu.SemaphoreType.DMA,
            pltpu.SemaphoreType.DMA((LEVELS + 1,)),
            pltpu.SemaphoreType.DMA((LEVELS, chunks)),
            pltpu.SemaphoreType.DMA((chunks,)),
        ],
        compiler_params=pltpu.CompilerParams(
            collective_id=0, has_side_effects=True, vmem_limit_bytes=48 * 2**20
        ),
        cost_estimate=pl.CostEstimate(
            flops=LEVELS * 2 * half * vecs * 4 * width * width,
            bytes_accessed=10 * 2**20,
            transcendentals=0,
        ),
    )(
        in_hbm(coefficients.reshape(2, half, vecs, width)),
        in_hbm(translations),
        in_hbm(box_gains.reshape(LEVELS, 2, half, width)),
    )
    return result.reshape(boxes, vecs, width)


def solution(mesh):
    return jax.shard_map(
        shards,
        mesh=mesh,
        in_specs=(P(("gx", "gy", "gz"), None, None), P(), P(None, ("gx", "gy", "gz"), None)),
        out_specs=P(("gx", "gy", "gz"), None, None),
        check_vma=False,
    )
```

time: 208 us -> 197 us (0.947)
  Pallas kernels: 204 us -> 195 us
  local copies, waits for them, and re-layouts: 4.28 us -> 2.02 us
    pallas_call x1, Pallas kernels: 204 us -> 195 us  [shards(): pl.pallas_call(butterfly, out_shape=pltpu.VMEM((2, half, vecs, width), bf...]
    unnamed x5 -> x1, local copies, waits for them, and re-layouts: 4.28 us -> 2.02 us
where the time goes in v2:
time: 197 us
  Pallas kernels  195 us (99%)
  local copies, waits for them, and re-layouts  2.02 us (1%)
    pallas_call x1, Pallas kernels, shards(): pl.pallas_call(butterfly, out_shape=pltpu.VMEM((2, half, vecs, width), bf...  195 us

profile of v2, /device:TPU:1, one launch (start us, length us, event | category | flops | bytes accessed | tf_op | source)
XLA Modules:
  0.0 196.8 jit_solution(16301054667320793528)
XLA Ops:
  0.0 194.7 %shard_map.37 = bf16[2,512,16,128]{3,2,1,0:T(8,128)(2,1)S(1)} custom-call(bf16[2,512,16,128]{3,2,1,0:T(8,128)(2,1)} %bitcast.4, bf16[4,2,2,128,128]{4,3,2,1,0:T(8,128)(2,1)} %blocks.1, bf16[4,2,512,128]{3,2,1,0:T(8,128)(2,1)} %bitcast.5), custom_call_target="tpu_custom_call" | custom-call | flops 4294967296 | bytes 10485760 | tf_op jit(solution)/shard_map/pallas_call | solution.py:188
  194.7 2.0 %copy.5 = bf16[1024,16,128]{2,1,0:T(8,128)(2,1)} copy(bf16[1024,16,128]{2,1,0:T(8,128)(2,1)S(1)} %bitcast.3) | data formatting | bytes 8388608

commit v3 on v2

--- a/solution.py
+++ b/solution.py
@@ -11,12 +11,12 @@
 LEVELS = 4
 SMALL = 16
 LARGE = 32
-HEAD = 2
+HEAD = 6
 TAIL = 2
 FIRST = 2
-AHEAD = 2
-LAGS = (0, 2, 7, 9)
-PASS_LAG = 4
+AHEAD = 3
+LAGS = (0, 2, 9, 11)
+PASS_LAG = 5
 
 
 def butterfly(

time: 197 us -> 196 us (level)
  no operation moved by 1% of the time
where the time goes in v3:
time: 196 us
  Pallas kernels  194 us (99%)
  local copies, waits for them, and re-layouts  2.02 us (1%)
    pallas_call x1, Pallas kernels, shards(): pl.pallas_call(butterfly, out_shape=pltpu.VMEM((2, half, vecs, width), bf...  194 us

profile of v3, /device:TPU:1, one launch (start us, length us, event | category | flops | bytes accessed | tf_op | source)
XLA Modules:
  0.0 196.2 jit_solution(16727237140245037944)
XLA Ops:
  0.0 194.2 %shard_map.37 = bf16[2,512,16,128]{3,2,1,0:T(8,128)(2,1)S(1)} custom-call(bf16[2,512,16,128]{3,2,1,0:T(8,128)(2,1)} %bitcast.4, bf16[4,2,2,128,128]{4,3,2,1,0:T(8,128)(2,1)} %blocks.1, bf16[4,2,512,128]{3,2,1,0:T(8,128)(2,1)} %bitcast.5), custom_call_target="tpu_custom_call" | custom-call | flops 4294967296 | bytes 10485760 | tf_op jit(solution)/shard_map/pallas_call | solution.py:188
  194.2 2.0 %copy.5 = bf16[1024,16,128]{2,1,0:T(8,128)(2,1)} copy(bf16[1024,16,128]{2,1,0:T(8,128)(2,1)S(1)} %bitcast.3) | data formatting | bytes 8388608

commit v4 on v3

--- a/solution.py
+++ b/solution.py
@@ -15,6 +15,7 @@
 TAIL = 2
 FIRST = 2
 AHEAD = 3
+REUSE = 8
 LAGS = (0, 2, 9, 11)
 PASS_LAG = 5
 
@@ -72,7 +73,7 @@
             src_ref=source,
             dst_ref=passing.at[part(chunk, size)] if level == 2 else arrived.at[level, part(chunk, size)],
             send_sem=send_sems.at[level],
-            recv_sem=pass_sems.at[chunk] if level == 2 else recv_sems.at[level, chunk],
+            recv_sem=pass_sems.at[0, chunk] if level == 2 else recv_sems.at[level - level // 3, chunk % REUSE],
             device_id=partners[level],
             device_id_type=MESH,
         )
@@ -82,7 +83,7 @@
             src_ref=passing.at[part(chunk, size)],
             dst_ref=arrived.at[2, part(chunk, size)],
             send_sem=send_sems.at[LEVELS],
-            recv_sem=recv_sems.at[2, chunk],
+            recv_sem=pass_sems.at[1, chunk],
             device_id=partners[2],
             device_id_type=MESH,
         )
@@ -203,8 +204,8 @@
             pltpu.SemaphoreType.DMA,
             pltpu.SemaphoreType.DMA,
             pltpu.SemaphoreType.DMA((LEVELS + 1,)),
-            pltpu.SemaphoreType.DMA((LEVELS, chunks)),
-            pltpu.SemaphoreType.DMA((chunks,)),
+            pltpu.SemaphoreType.DMA((LEVELS - 1, REUSE)),
+            pltpu.SemaphoreType.DMA((2, chunks)),
         ],
         compiler_params=pltpu.CompilerParams(
             collective_id=0, has_side_effects=True, vmem_limit_bytes=48 * 2**20

time: 196 us -> 196 us (level)
  no operation moved by 1% of the time
where the time goes in v4:
time: 196 us
  Pallas kernels  194 us (99%)
  local copies, waits for them, and re-layouts  2.02 us (1%)
    pallas_call x1, Pallas kernels, shards(): pl.pallas_call(butterfly, out_shape=pltpu.VMEM((2, half, vecs, width), bf...  194 us

profile of v4, /device:TPU:1, one launch (start us, length us, event | category | flops | bytes accessed | tf_op | source)
XLA Modules:
  0.0 195.9 jit_solution(15356751491583508745)
XLA Ops:
  0.0 193.9 %shard_map.37 = bf16[2,512,16,128]{3,2,1,0:T(8,128)(2,1)S(1)} custom-call(bf16[2,512,16,128]{3,2,1,0:T(8,128)(2,1)} %bitcast.4, bf16[4,2,2,128,128]{4,3,2,1,0:T(8,128)(2,1)} %blocks.1, bf16[4,2,512,128]{3,2,1,0:T(8,128)(2,1)} %bitcast.5), custom_call_target="tpu_custom_call" | custom-call | flops 4294967296 | bytes 10485760 | tf_op jit(solution)/shard_map/pallas_call | solution.py:189
  193.9 2.0 %copy.5 = bf16[1024,16,128]{2,1,0:T(8,128)(2,1)} copy(bf16[1024,16,128]{2,1,0:T(8,128)(2,1)S(1)} %bitcast.3) | data formatting | bytes 8388608

commit v5 on v4

--- a/solution.py
+++ b/solution.py
@@ -14,7 +14,7 @@
 HEAD = 6
 TAIL = 2
 FIRST = 2
-AHEAD = 3
+AHEAD = 2
 REUSE = 8
 LAGS = (0, 2, 9, 11)
 PASS_LAG = 5
@@ -27,10 +27,15 @@
 ):
     gx, gy, gz = lax.axis_index("gx"), lax.axis_index("gy"), lax.axis_index("gz")
     sides = (gx % 2, gz % 2, gz // 2, gy % 2)
+
+    def along(steps):
+        place = (2 * gz + sides[0] + steps) % 8
+        return {"gx": gx - sides[0] + place % 2, "gz": place // 2}
+
     partners = (
         {"gx": gx + 1 - 2 * sides[0]},
         {"gz": gz + 1 - 2 * sides[1]},
-        {"gz": (gz + 1 + 2 * sides[3]) % 4},
+        along(3 * (1 + 6 * sides[3])),
         {"gy": gy + 1 - 2 * sides[3]},
     )
     half, vecs, width = own.shape
@@ -84,7 +89,7 @@
             dst_ref=arrived.at[2, part(chunk, size)],
             send_sem=send_sems.at[LEVELS],
             recv_sem=pass_sems.at[1, chunk],
-            device_id=partners[2],
+            device_id=along(1 + 6 * sides[3]),
             device_id_type=MESH,
         )
 
@@ -97,9 +102,9 @@
             load_gains(level, place).start()
 
     barrier = pltpu.get_barrier_semaphore()
-    for peer in (partners[0], {"gz": (gz + 1) % 4}, {"gz": (gz + 3) % 4}, partners[3]):
+    for peer in (along(1), along(3), along(5), along(7), partners[1], partners[3]):
         pl.semaphore_signal(barrier, inc=1, device_id=peer, device_id_type=MESH)
-    pl.semaphore_wait(barrier, 4)
+    pl.semaphore_wait(barrier, 6)
 
     for chunk in range(FIRST):
         exchange(0, chunk, SMALL if chunk < HEAD else LARGE).start()

time: 196 us -> 196 us (level)
  no operation moved by 1% of the time
where the time goes in v5:
time: 196 us
  Pallas kernels  194 us (99%)
  local copies, waits for them, and re-layouts  2.02 us (1%)
    pallas_call x1, Pallas kernels, shards(): pl.pallas_call(butterfly, out_shape=pltpu.VMEM((2, half, vecs, width), bf...  194 us

profile of v5, /device:TPU:1, one launch (start us, length us, event | category | flops | bytes accessed | tf_op | source)
XLA Modules:
  0.0 195.6 jit_solution(1672491887377549078)
XLA Ops:
  0.0 193.6 %shard_map.37 = bf16[2,512,16,128]{3,2,1,0:T(8,128)(2,1)S(1)} custom-call(bf16[2,512,16,128]{3,2,1,0:T(8,128)(2,1)} %bitcast.4, bf16[4,2,2,128,128]{4,3,2,1,0:T(8,128)(2,1)} %blocks.1, bf16[4,2,512,128]{3,2,1,0:T(8,128)(2,1)} %bitcast.5), custom_call_target="tpu_custom_call" | custom-call | flops 4294967296 | bytes 10485760 | tf_op jit(solution)/shard_map/pallas_call | solution.py:194
  193.6 2.0 %copy.5 = bf16[1024,16,128]{2,1,0:T(8,128)(2,1)} copy(bf16[1024,16,128]{2,1,0:T(8,128)(2,1)S(1)} %bitcast.3) | data formatting | bytes 8388608
